TPU v7x, 256 devices: a whole 4x4x8 slice. The times are simulated.
256 devices in a mesh: segment: 4 (over y), seq: 64 (over z, x, core).
Axes of the slice: x: 4, y: 4, z: 8, core: 2. Of those that a mesh axis runs over, the one named last changes fastest.
Arguments:
- queries: bfloat16 [4, 8192, 4096], P('segment', 'seq'), as said below
- cache: bfloat16 [4, 2, 32768, 256], P('segment', None, 'seq'), as said below
- packed: bfloat16 [4, 2, 1024, 256], P('segment', None, 'seq'), as said below
- fresh: bfloat16 [4, 8192, 2, 256], P('segment', 'seq'), as said below
- gates: bfloat16 [4, 8192, 96], P('segment', 'seq'), may hold values from -4 to 4
- chosen: int32 [4, 128, 2, 16], P('segment', 'seq'), may hold values from 0 to 511, as said below
Outputs:
- handed: bfloat16 [4, 8192, 4096], P('segment', 'seq')
Inputs may be any that keep to these rules, and one draw needn't show every extreme that they name: `chosen`: within one query block and KV head the 16 entries are different blocks of 64 positions. Over both KV heads, at most 2 of the selections of one device's query blocks fall in the cached blocks of one index of seq, and some device reaches 2 for one index of seq within one KV head. `queries`: Real-valued entries. `cache`: Real-valued entries. `packed`: Real-valued entries. `fresh`: Real-valued entries.
All inputs are finite; a program needn't handle non-finite values.
Results may differ from a plain program's by a relative error of at most 0.0045.
Values may be sent and summed in bfloat16 or wider, within the bound.
A program may use at most 128 MiB of HBM per device.

v0:
```python
import jax
import jax.numpy as jnp
from jax import lax
from jax.sharding import PartitionSpec as P

HEAD_SIZE = 128
KEY_HEADS = 2
QUERY_PER_KEY = 16
SELECT_SPAN = 64
PICKED_BLOCKS = 16
WINDOW_LENGTH = 512


score_after_mask = -1e30


def from_behind(value, axis, steps):
    count = lax.axis_size(axis)
    leading, last = (max(0, -steps), min(count, count - steps))
    return lax.ppermute(value, axis, [(source, source + steps) for source in range(leading, last)])


def passed_along(value, axis, steps):
    count = lax.axis_size(axis)
    pairs = [(source, (source + steps) % count) for source in range(count)]
    return lax.ppermute(value, axis, pairs)


def attend_branch(query_vector, keys, values, inside, score_form, mix_form):
    scores = jnp.einsum(
        score_form, query_vector, keys, preferred_element_type=jnp.float32
    ) * HEAD_SIZE ** (-0.5)
    if inside is not None:
        scores = jnp.where(inside, scores, score_after_mask)
    row_peak = jnp.max(scores, axis=-1, keepdims=True)
    weights = jnp.exp(scores - row_peak).astype(jnp.bfloat16)
    softmax_denominator = jnp.sum(weights.astype(jnp.float32), axis=-1)
    softmax_numerator = jnp.einsum(mix_form, weights, values, preferred_element_type=jnp.float32)
    return softmax_numerator / softmax_denominator[..., None]


def fetch_blocks(block_codes, owner_parts, block_table, slot_capacity, sequence_parts):
    owner_hits = (
        owner_parts[:, None] == jnp.arange(sequence_parts, dtype=jnp.int32)[None, :]
    ).astype(jnp.int32)
    slot_rank = jnp.sum((jnp.cumsum(owner_hits, axis=0) - owner_hits) * owner_hits, axis=1)
    requests = (
        jnp.full((sequence_parts, slot_capacity), -1, jnp.int32)
        .at[owner_parts, slot_rank]
        .set(block_codes)
    )
    served = jnp.take(
        block_table,
        jnp.maximum(lax.all_to_all(requests, "seq", split_axis=0, concat_axis=0, tiled=True), 0),
        axis=0,
    )
    returned = lax.all_to_all(served, "seq", split_axis=0, concat_axis=0, tiled=True)
    return returned[owner_parts, slot_rank]


def per_device(queries, cache, packed, fresh, gates, chosen):
    tokens_per_part = queries.shape[1]
    blocks_per_part = tokens_per_part // SELECT_SPAN
    sequence_parts = lax.axis_size("seq")
    device_index = lax.axis_index("seq")
    per_owner_part = cache.shape[2] // SELECT_SPAN
    slot_capacity = max(
        2, min(per_owner_part, 2 * blocks_per_part * KEY_HEADS * PICKED_BLOCKS // sequence_parts)
    )
    query_vector = queries[0].reshape(tokens_per_part, KEY_HEADS, QUERY_PER_KEY, HEAD_SIZE)
    portion = lax.all_gather(packed[0], "seq", axis=1, tiled=True)
    running_maximum = jnp.full(
        (tokens_per_part, KEY_HEADS, QUERY_PER_KEY), score_after_mask, jnp.float32
    )
    softmax_denominator = jnp.zeros((tokens_per_part, KEY_HEADS, QUERY_PER_KEY), jnp.float32)
    softmax_numerator = jnp.zeros(
        (tokens_per_part, KEY_HEADS, QUERY_PER_KEY, HEAD_SIZE), jnp.float32
    )
    entry_count = portion.shape[1]
    for sub_begin in range(0, entry_count, 512):
        sub_portion = portion[:, sub_begin : sub_begin + 512]
        scores = jnp.einsum(
            "tghd,gcd->tghc",
            query_vector,
            sub_portion[..., :HEAD_SIZE],
            preferred_element_type=jnp.float32,
        ) * HEAD_SIZE ** (-0.5)
        new_max = jnp.maximum(running_maximum, jnp.max(scores, axis=-1))
        weights = jnp.exp(scores - new_max[..., None]).astype(jnp.bfloat16)
        shrink = jnp.exp(running_maximum - new_max)
        softmax_denominator = softmax_denominator * shrink + jnp.sum(
            weights.astype(jnp.float32), axis=-1
        )
        softmax_numerator = softmax_numerator * shrink[..., None] + jnp.einsum(
            "tghc,gcd->tghd",
            weights,
            sub_portion[..., HEAD_SIZE:],
            preferred_element_type=jnp.float32,
        )
        running_maximum = new_max
    running_maximum, softmax_denominator, softmax_numerator = (
        running_maximum,
        softmax_denominator,
        softmax_numerator,
    )
    summary = softmax_numerator / softmax_denominator[..., None]
    chosen_local = chosen[0]
    owners_all = chosen_local // per_owner_part
    local_all = chosen_local % per_owner_part
    per_head = []
    for key_value_head in range(KEY_HEADS):
        block_table = cache[0, key_value_head].reshape(per_owner_part, SELECT_SPAN, 2 * HEAD_SIZE)
        gathered = fetch_blocks(
            local_all[:, key_value_head].reshape(-1),
            owners_all[:, key_value_head].reshape(-1),
            block_table,
            slot_capacity,
            sequence_parts,
        )
        per_head.append(
            gathered.reshape(blocks_per_part, PICKED_BLOCKS * SELECT_SPAN, 2 * HEAD_SIZE)
        )
    selected_kv = jnp.stack(per_head, axis=1)
    own_keys = fresh[0]
    reach_devices = -(-WINDOW_LENGTH // tokens_per_part)
    earlier_keys = [
        from_behind(own_keys, "seq", distance) for distance in range(reach_devices, 0, -1)
    ]
    window_keys = jnp.concatenate(earlier_keys + [own_keys], axis=0)
    blocks_of_query = query_vector.reshape(
        blocks_per_part, SELECT_SPAN, KEY_HEADS, QUERY_PER_KEY, HEAD_SIZE
    )

    def block_local(inputs):
        index_of_block, query_block, picked_key_value = inputs
        picked = attend_branch(
            query_block,
            picked_key_value[..., :HEAD_SIZE],
            picked_key_value[..., HEAD_SIZE:],
            None,
            "tghd,gkd->tghk",
            "tghk,gkd->tghd",
        )
        first_row = reach_devices * tokens_per_part + index_of_block * SELECT_SPAN - WINDOW_LENGTH
        near = lax.dynamic_slice_in_dim(window_keys, first_row, WINDOW_LENGTH + SELECT_SPAN, 0)
        block_start = device_index * tokens_per_part + index_of_block * SELECT_SPAN
        query_pos = block_start + jnp.arange(SELECT_SPAN, dtype=jnp.int32)
        key_pos = (
            block_start - WINDOW_LENGTH + jnp.arange(WINDOW_LENGTH + SELECT_SPAN, dtype=jnp.int32)
        )
        inside = (
            (key_pos[None, :] <= query_pos[:, None])
            & (key_pos[None, :] > query_pos[:, None] - WINDOW_LENGTH)
            & (key_pos[None, :] >= 0)
        )
        local = attend_branch(
            query_block,
            near[..., :HEAD_SIZE],
            near[..., HEAD_SIZE:],
            inside[:, None, None, :],
            "tghd,kgd->tghk",
            "tghk,kgd->tghd",
        )
        return (picked, local)

    all_picked_rows, every_head_local = lax.map(
        block_local, (jnp.arange(blocks_per_part, dtype=jnp.int32), blocks_of_query, selected_kv)
    )
    all_picked_rows = all_picked_rows.reshape(tokens_per_part, KEY_HEADS, QUERY_PER_KEY, HEAD_SIZE)
    every_head_local = every_head_local.reshape(
        tokens_per_part, KEY_HEADS, QUERY_PER_KEY, HEAD_SIZE
    )
    gate_values = jax.nn.sigmoid(gates[0].astype(jnp.float32)).reshape(
        tokens_per_part, 3, KEY_HEADS, QUERY_PER_KEY, 1
    )
    combined_output = (
        gate_values[:, 0] * summary
        + gate_values[:, 1] * all_picked_rows
        + gate_values[:, 2] * every_head_local
    )
    attended_output = combined_output.reshape(
        1, tokens_per_part, KEY_HEADS * QUERY_PER_KEY * HEAD_SIZE
    ).astype(jnp.bfloat16)
    return passed_along(attended_output, "segment", 1)


def solution(mesh):
    placed = (
        P("segment", "seq", None),
        P("segment", None, "seq", None),
        P("segment", None, "seq", None),
        P("segment", "seq", None, None),
        P("segment", "seq", None),
        P("segment", "seq", None, None),
    )
    return jax.shard_map(
        per_device, mesh=mesh, in_specs=placed, out_specs=P("segment", "seq", None), check_vma=False
    )
```

profile of v0, /device:TPU:32, one launch (start us, length us, event | category | flops | bytes accessed | tf_op | source)
XLA Modules:
  0.0 371.7 jit_solution(14197082724497110580)
XLA Ops:
  7.8 2.0 scatter_fusion
  10.6 11.6 %all-to-all-start = ((s32[64,1,2]{2,1,0:T(1,128)}), s32[64,1,2]{2,1,0:T(1,128)S(1)}, u32[]{:S(2)}, u32[]{:S(2)}) async-start(s32[64,1,2]{2,1,0:T(1,128)} %copy.76), calls=%async_computation | async-start | bytes 65536 | tf_op jit(solution)/shard_map/all_to_all | solution.py:54
  23.8 2.0 scatter_fusion.1
  26.6 4.2 %all-to-all-done = s32[64,1,2]{2,1,0:T(1,128)S(1)} async-done(((s32[64,1,2]{2,1,0:T(1,128)}), s32[64,1,2]{2,1,0:T(1,128)S(1)}, u32[]{:S(2)}, u32[]{:S(2)}) %all-to-all-start) | async-done | bytes 544 | tf_op jit(solution)/shard_map/all_to_all | solution.py:54
  30.8 6.1 %all-to-all-start.2 = ((s32[64,1,2]{2,1,0:T(1,128)}), s32[64,1,2]{2,1,0:T(1,128)S(1)}, u32[]{:S(2)}, u32[]{:S(2)}) async-start(s32[64,1,2]{2,1,0:T(1,128)} %copy.80), calls=%async_computation.2 | async-start | bytes 65536 | tf_op jit(solution)/shard_map/all_to_all | solution.py:54
  37.3 2.8 gather_fusion.2
  40.1 4.6 %broadcast_select_fusion.1 = bf16[64,2,64,256]{3,2,1,0:T(8,128)(2,1)} fusion(bf16[64,2,64,256]{3,2,1,0:T(8,128)(2,1)} %bitcast.263, pred[64,2]{1,0:T(8,128)(4,1)S(1)} %copy.78), kind=kLoop, calls=%fused_computation.53 | loop fusion | flops 2097152 | bytes 8388736 | tf_op jit(solution)/shard_map/jit(_take)/select_n | solution.py:52
  45.4 9.8 %all-to-all-start.1 = ((bf16[64,2,64,256]{3,2,1,0:T(8,128)(2,1)}), bf16[64,2,64,256]{3,2,1,0:T(8,128)(2,1)}, u32[]{:S(2)}, u32[]{:S(2)}) async-start(bf16[64,2,64,256]{3,2,1,0:T(8,128)(2,1)} %broadcast_select_fusion.1), calls=%async_computation.1 | async-start | bytes 8388608 | tf_op jit(solution)/shard_map/all_to_all | solution.py:57
  55.6 2.8 gather_fusion.3
  58.4 4.6 %broadcast_select_fusion = bf16[64,2,64,256]{3,2,1,0:T(8,128)(2,1)} fusion(bf16[64,2,64,256]{3,2,1,0:T(8,128)(2,1)} %bitcast.264, pred[64,2]{1,0:T(8,128)(4,1)S(1)} %copy.82), kind=kLoop, calls=%fused_computation.52 | loop fusion | flops 2097152 | bytes 8388736 | tf_op jit(solution)/shard_map/jit(_take)/select_n | solution.py:52
  63.0 87.4 %all-to-all-done.1 = bf16[64,2,64,256]{3,2,1,0:T(8,128)(2,1)} async-done(((bf16[64,2,64,256]{3,2,1,0:T(8,128)(2,1)}), bf16[64,2,64,256]{3,2,1,0:T(8,128)(2,1)}, u32[]{:S(2)}, u32[]{:S(2)}) %all-to-all-start.1) | async-done | bytes 4194336 | tf_op jit(solution)/shard_map/all_to_all | solution.py:57
  150.4 6.6 %all-to-all-start.3 = ((bf16[64,2,64,256]{3,2,1,0:T(8,128)(2,1)}), bf16[64,2,64,256]{3,2,1,0:T(8,128)(2,1)}, u32[]{:S(2)}, u32[]{:S(2)}) async-start(bf16[64,2,64,256]{3,2,1,0:T(8,128)(2,1)} %broadcast_select_fusion), calls=%async_computation.3 | async-start | bytes 8388608 | tf_op jit(solution)/shard_map/all_to_all | solution.py:57
  157.8 4.9 %collective-permute-start = (bf16[128,2,256]{2,0,1:T(8,128)(2,1)S(1)}, bf16[128,2,256]{2,0,1:T(8,128)(2,1)S(1)}, u32[]{:S(2)}, u32[]{:S(2)}) collective-permute-start(bf16[128,2,256]{2,0,1:T(8,128)(2,1)S(1)} %bitcast.278), channel_id=1, source_target_pairs={{0,4},{1,5},{2,6},{3,7},{4,8},{5,9},{6,10},{7,11},{8,12},{9,13},{1... | collective-permute-start | bytes 393224 | tf_op jit(solution)/shard_map/ppermute | solution.py:20
  164.6 2.8 collective-permute-start.2
  167.4 3.8 %collective-permute-start.3 = (bf16[128,2,256]{2,0,1:T(8,128)(2,1)S(1)}, bf16[128,2,256]{2,0,1:T(8,128)(2,1)S(1)}, u32[]{:S(2)}, u32[]{:S(2)}) collective-permute-start(bf16[128,2,256]{2,0,1:T(8,128)(2,1)S(1)} %bitcast.281), channel_id=1, source_target_pairs={{0,1},{1,2},{2,3},{3,4},{4,5},{5,6},{6,7},{7,8},{8,9},{9,10},{10,1... | collective-permute-start | bytes 393224 | tf_op jit(solution)/shard_map/ppermute | solution.py:20
  171.6 85.2 %collective-permute-done = bf16[128,2,256]{2,0,1:T(8,128)(2,1)S(1)} collective-permute-done((bf16[128,2,256]{2,0,1:T(8,128)(2,1)S(1)}, bf16[128,2,256]{2,0,1:T(8,128)(2,1)S(1)}, u32[]{:S(2)}, u32[]{:S(2)}) %collective-permute-start) | collective-permute-done | bytes 131104 | tf_op jit(solution)/shard_map/ppermute | solution.py:20
  258.9 3.4 collective-permute-done.2
  264.5 2.3 bitcast_reduce_fusion.2
  268.2 3.3 convert_reduce_fusion.2
  271.5 3.0 fusion.29
  274.5 2.8 gather_fusion
  277.3 2.8 gather_fusion.1
  281.6 43.9 %while.17 = (s32[]{:T(128)}, f32[2,64,2,16,128]{4,3,2,1,0:T(8,128)}, f32[2,64,2,16,128]{4,3,2,1,0:T(8,128)}, bf16[2,2,1024,256]{3,2,1,0:T(8,128)(2,1)}, bf16[2,6...) while((s32[]{:T(128)}, ...), condition=%wide.region_15.17_spmd, body=%wide.region_10.16_spmd.sunk | while | flops 1714694016 | bytes 104651792 | solution.py:166
  289.2 2.3 fusion.49
  291.6 2.4 copy-done
  295.4 4.0 %fusion.50 = f32[1,64,2,16,128]{4,1,3,2,0:T(8,128)S(1)} fusion(f32[64,2,16]{0,2,1:T(8,128)S(1)} %convert_reduce_fusion.6, bf16[640,2,256]{2,0,1:T(8,128)(2,1)} %get-tuple-element.369, s32[]{:T(128)S(6)} %select_n.145, s32[]{:T(128)S(6)} %add.347, f32[2,576,64,16]{1,2,3,0:T(8,128)} %copy-done, f32[64,2,16]{0,2,1:T(8,128)S(1)} %get-tuple-element.329, ...), kind=kOutput, calls=%fused_computation.17.clone.1 | convolution fusion | flops 306970624 | bytes 6639624 | tf_op jit(solution)/shard_map/while/body/eval_jaxpr/tghk,kgd->tghd/dot_general | solution.py:38
  311.1 2.3 fusion.49
  313.5 2.4 copy-done
  317.3 4.0 %fusion.50 = f32[1,64,2,16,128]{4,1,3,2,0:T(8,128)S(1)} fusion(f32[64,2,16]{0,2,1:T(8,128)S(1)} %convert_reduce_fusion.6, bf16[640,2,256]{2,0,1:T(8,128)(2,1)} %get-tuple-element.369, s32[]{:T(128)S(6)} %select_n.145, s32[]{:T(128)S(6)} %add.347, f32[2,576,64,16]{1,2,3,0:T(8,128)} %copy-done, f32[64,2,16]{0,2,1:T(8,128)S(1)} %get-tuple-element.329, ...), kind=kOutput, calls=%fused_computation.17.clone.1 | convolution fusion | flops 306970624 | bytes 6639624 | tf_op jit(solution)/shard_map/while/body/eval_jaxpr/tghk,kgd->tghd/dot_general | solution.py:38
  325.5 3.1 copy.87
  330.5 7.6 %fusion.24 = bf16[128,2,16,128]{0,3,2,1:T(8,128)(2,1)S(1)} fusion(f32[128,2,16,128]{0,3,2,1:T(8,128)} %copy.90, f32[128,2,16,128]{0,3,2,1:T(8,128)} %copy.87, f32[2,128,16,128]{1,3,2,0:T(8,128)} %fusion.29, f32[128,2,16]{0,2,1:T(8,128)S(1)} %get-tuple-element.255, f32[128,2,16]{0,2,1:T(8,128)S(1)} %get-tuple-element.256, ...), kind=kOutput, calls=%fused_computation.62 | convolution fusion | flops 548405248 | bytes 16105472 | tf_op jit(solution)/shard_map/tghc,gcd->tghd/dot_general | solution.py:94
  340.3 23.6 %collective-permute-done.4 = bf16[1,128,4096]{2,1,0:T(8,128)(2,1)S(1)} collective-permute-done((bf16[1,128,4096]{2,1,0:T(8,128)(2,1)S(1)}, bf16[1,128,4096]{2,1,0:T(8,128)(2,1)S(1)}, u32[]{:S(2)}, u32[]{:S(2)}) %collective-permute-start.4) | collective-permute-done | bytes 1048608 | tf_op jit(solution)/shard_map/ppermute | solution.py:26
  (119 shorter events, 46.2 us)
Async XLA Ops:
  10.6 20.2 %all-to-all-start = ((s32[64,1,2]{2,1,0:T(1,128)}), s32[64,1,2]{2,1,0:T(1,128)S(1)}, u32[]{:S(2)}, u32[]{:S(2)}) async-start(s32[64,1,2]{2,1,0:T(1,128)} %copy.76), calls=%async_computation | async-start | bytes 65536 | tf_op jit(solution)/shard_map/all_to_all | solution.py:54
  30.8 14.6 %all-to-all-start.2 = ((s32[64,1,2]{2,1,0:T(1,128)}), s32[64,1,2]{2,1,0:T(1,128)S(1)}, u32[]{:S(2)}, u32[]{:S(2)}) async-start(s32[64,1,2]{2,1,0:T(1,128)} %copy.80), calls=%async_computation.2 | async-start | bytes 65536 | tf_op jit(solution)/shard_map/all_to_all | solution.py:54
  45.4 105.0 %all-to-all-start.1 = ((bf16[64,2,64,256]{3,2,1,0:T(8,128)(2,1)}), bf16[64,2,64,256]{3,2,1,0:T(8,128)(2,1)}, u32[]{:S(2)}, u32[]{:S(2)}) async-start(bf16[64,2,64,256]{3,2,1,0:T(8,128)(2,1)} %broadcast_select_fusion.1), calls=%async_computation.1 | async-start | bytes 8388608 | tf_op jit(solution)/shard_map/all_to_all | solution.py:57
  63.0 94.7 %copy-start.9 = (bf16[1,128,2,256]{3,2,1,0:T(2,128)(2,1)S(1)}, bf16[1,128,2,256]{3,2,1,0:T(2,128)(2,1)}, u32[]{:S(2)}) copy-start(bf16[1,128,2,256]{3,2,1,0:T(2,128)(2,1)} %param.13) | copy-start | bytes 393220
  63.0 108.2 %copy-start.10 = (bf16[1,128,96]{1,2,0:T(8,128)(2,1)S(1)}, bf16[1,128,96]{1,2,0:T(8,128)(2,1)}, u32[]{:S(2)}) copy-start(bf16[1,128,96]{1,2,0:T(8,128)(2,1)} %param.14) | copy-start | bytes 73732
  63.0 108.3 %copy-start.7 = (bf16[1,128,4096]{2,1,0:T(8,128)(2,1)S(1)}, bf16[1,128,4096]{2,1,0:T(8,128)(2,1)}, u32[]{:S(2)}) copy-start(bf16[1,128,4096]{2,1,0:T(8,128)(2,1)} %param.10) | copy-start | bytes 3145732
  150.4 126.9 %all-to-all-start.3 = ((bf16[64,2,64,256]{3,2,1,0:T(8,128)(2,1)}), bf16[64,2,64,256]{3,2,1,0:T(8,128)(2,1)}, u32[]{:S(2)}, u32[]{:S(2)}) async-start(bf16[64,2,64,256]{3,2,1,0:T(8,128)(2,1)} %broadcast_select_fusion), calls=%async_computation.3 | async-start | bytes 8388608 | tf_op jit(solution)/shard_map/all_to_all | solution.py:57
  157.0 107.5 %all-gather.3.cloned.1.call-start = ((), (), s32[]{:S(2)}) async-start(), calls=%async_computation.4 | async-start | bytes 1064960 | tf_op jit(solution)/shard_map/all_gather | solution.py:71
  157.8 99.0 %collective-permute-start = (bf16[128,2,256]{2,0,1:T(8,128)(2,1)S(1)}, bf16[128,2,256]{2,0,1:T(8,128)(2,1)S(1)}, u32[]{:S(2)}, u32[]{:S(2)}) collective-permute-start(bf16[128,2,256]{2,0,1:T(8,128)(2,1)S(1)} %bitcast.278), channel_id=1, source_target_pairs={{0,4},{1,5},{2,6},{3,7},{4,8},{5,9},{6,10},{7,11},{8,12},{9,13},{1... | collective-permute-start | bytes 393224 | tf_op jit(solution)/shard_map/ppermute | solution.py:20
  162.7 95.5 %collective-permute-start.1 = (bf16[128,2,256]{2,0,1:T(8,128)(2,1)S(1)}, bf16[128,2,256]{2,0,1:T(8,128)(2,1)S(1)}, u32[]{:S(2)}, u32[]{:S(2)}) collective-permute-start(bf16[128,2,256]{2,0,1:T(8,128)(2,1)S(1)} %bitcast.279), channel_id=1, source_target_pairs={{0,3},{1,4},{2,5},{3,6},{4,7},{5,8},{6,9},{7,10},{8,11},{9,12},{10... | collective-permute-start | bytes 393224 | tf_op jit(solution)/shard_map/ppermute | solution.py:20
  164.6 97.6 %collective-permute-start.2 = (bf16[128,2,256]{2,0,1:T(8,128)(2,1)S(1)}, bf16[128,2,256]{2,0,1:T(8,128)(2,1)S(1)}, u32[]{:S(2)}, u32[]{:S(2)}) collective-permute-start(bf16[128,2,256]{2,0,1:T(8,128)(2,1)S(1)} %bitcast.280), channel_id=1, source_target_pairs={{0,2},{1,3},{2,4},{3,5},{4,6},{5,7},{6,8},{7,9},{8,10},{9,11},{10,... | collective-permute-start | bytes 393224 | tf_op jit(solution)/shard_map/ppermute | solution.py:20
  167.4 95.8 %collective-permute-start.3 = (bf16[128,2,256]{2,0,1:T(8,128)(2,1)S(1)}, bf16[128,2,256]{2,0,1:T(8,128)(2,1)S(1)}, u32[]{:S(2)}, u32[]{:S(2)}) collective-permute-start(bf16[128,2,256]{2,0,1:T(8,128)(2,1)S(1)} %bitcast.281), channel_id=1, source_target_pairs={{0,1},{1,2},{2,3},{3,4},{4,5},{5,6},{6,7},{7,8},{8,9},{9,10},{10,1... | collective-permute-start | bytes 393224 | tf_op jit(solution)/shard_map/ppermute | solution.py:20
  264.5 2.3 copy-start.8
  268.2 3.3 copy-start.1
  291.6 2.4 copy-start
  295.4 4.0 %copy-start.2 = (f32[2,64,2,16,128]{4,3,2,1,0:T(8,128)S(1)}, f32[2,64,2,16,128]{4,3,2,1,0:T(8,128)}, u32[]{:S(2)}) copy-start(f32[2,64,2,16,128]{4,3,2,1,0:T(8,128)} %get-tuple-element.350) | copy-start | bytes 6291460 | tf_op jit(solution)/shard_map/while
  295.4 4.0 %copy-start.4 = (f32[2,64,2,16,128]{4,3,2,1,0:T(8,128)S(1)}, f32[2,64,2,16,128]{4,3,2,1,0:T(8,128)}, u32[]{:S(2)}) copy-start(f32[2,64,2,16,128]{4,3,2,1,0:T(8,128)} %get-tuple-element.351) | copy-start | bytes 6291460 | tf_op jit(solution)/shard_map/while
  300.8 1.3 copy-start.3
  302.2 1.4 copy-start.5
  313.5 2.4 copy-start
  317.3 4.0 %copy-start.2 = (f32[2,64,2,16,128]{4,3,2,1,0:T(8,128)S(1)}, f32[2,64,2,16,128]{4,3,2,1,0:T(8,128)}, u32[]{:S(2)}) copy-start(f32[2,64,2,16,128]{4,3,2,1,0:T(8,128)} %get-tuple-element.350) | copy-start | bytes 6291460 | tf_op jit(solution)/shard_map/while
  317.3 4.0 %copy-start.4 = (f32[2,64,2,16,128]{4,3,2,1,0:T(8,128)S(1)}, f32[2,64,2,16,128]{4,3,2,1,0:T(8,128)}, u32[]{:S(2)}) copy-start(f32[2,64,2,16,128]{4,3,2,1,0:T(8,128)} %get-tuple-element.351) | copy-start | bytes 6291460 | tf_op jit(solution)/shard_map/while
  322.7 1.3 copy-start.3
  324.1 1.4 copy-start.5
  325.5 3.2 copy-start.6
  338.6 25.3 %collective-permute-start.4 = (bf16[1,128,4096]{2,1,0:T(8,128)(2,1)S(1)}, bf16[1,128,4096]{2,1,0:T(8,128)(2,1)S(1)}, u32[]{:S(2)}, u32[]{:S(2)}) collective-permute-start(bf16[1,128,4096]{2,1,0:T(8,128)(2,1)S(1)} %copy.91), channel_id=1, source_target_pairs={{0,64},{64,128},{128,192},{192,0},{1,65},{65,129},{129,193},{193,1... | collective-permute-start | bytes 3145736 | tf_op jit(solution)/shard_map/ppermute | solution.py:26
Sparse Core Ops, SparseCore 0:
  160.5 87.4 all-gather.2
where the time goes:
time: 372 us
  waiting for transfers between devices  206 us (55%)
  starting transfers between devices  49.1 us (13%)
  local copies, waits for them, and re-layouts  46 us (12%)
  matrix products  32.8 us (9%)
  other arithmetic  22.2 us (6%)
  between operations  13.7 us (4%)
    ppermute x4, waiting for transfers between devices, from_behind(): lax.ppermute(value, axis, [(source, source + steps) for source in range(l...  89.6 us
    all_to_all x2, waiting for transfers between devices, fetch_blocks(): lax.all_to_all(served, 'seq', split_axis=0, concat_axis=0, tiled=True)  87.4 us
    ppermute x1, waiting for transfers between devices, passed_along(): return lax.ppermute(value, axis, pairs)  23.6 us
    all_to_all x2, starting transfers between devices, fetch_blocks(): lax.all_to_all(requests, 'seq', split_axis=0, concat_axis=0, tiled=True)  17.7 us
    all_to_all x2, starting transfers between devices, fetch_blocks(): lax.all_to_all(served, 'seq', split_axis=0, concat_axis=0, tiled=True)  16.3 us
    ppermute x4, starting transfers between devices, from_behind(): lax.ppermute(value, axis, [(source, source + steps) for source in range(l...  13.4 us
    dot_general x4, matrix products, attend_branch(): jnp.einsum(mix_form, weights, values, preferred_element_type=jnp.float32)  11.4 us
    dot_general x2, matrix products, per_device(): jnp.einsum('tghc,gcd->tghd', weights, sub_portion[..., HEAD_SIZE:], prefe...  10.5 us
  transfers between devices with their start and end apart: 10, of which 8 were waited for; matrix products, arithmetic and copies ran while one was open for 10% of the time, Pallas kernels for 0%

commit v1 on v0

v1 whole, which is shorter than its diff:
```python
import functools

import jax
import jax.numpy as jnp
from jax import lax
from jax.experimental import pallas as pl
from jax.experimental.pallas import tpu as pltpu
from jax.sharding import PartitionSpec as P

HEAD = 128
KV_HEADS = 2
GROUP = 16
SPAN = 64
PICKED = 16
TOKENS = 128
WIDE = KV_HEADS * GROUP * HEAD
Z, X, C = 8, 4, 2
ROW = X * C
PARTS = Z * ROW
SECTIONS = 4
REACH = 4
MESH = pl.DeviceIdType.MESH
MASKED = -1e30
EXP_SCALE = HEAD**-0.5 * 1.4426950408889634


def dot_nt(a, b):
    return lax.dot_general(a, b, (((1,), (1,)), ((), ())), preferred_element_type=jnp.float32)


def dot_nn(a, b):
    return lax.dot_general(a, b, (((1,), (0,)), ((), ())), preferred_element_type=jnp.float32)


def with_ones(v):
    return jnp.concatenate([v, jnp.ones(v.shape, v.dtype)], axis=1)


def request_tile(chosen_row):
    lane = lax.broadcasted_iota(jnp.int32, (128, 128), 1)
    down = lax.broadcasted_iota(jnp.int32, (128, 128), 0)
    across = jnp.broadcast_to(chosen_row, (128, 128))
    column = across.T
    owner_across = lax.shift_right_logical(across, 3)
    owner_down = lax.shift_right_logical(column, 3)
    head_down = lax.shift_right_logical(down, 4) & 1
    code_down = (column & 7) + 8 * head_down
    key_down = down * 16 + code_down
    mine = owner_down == lane
    first = jnp.min(jnp.where(mine, key_down, 1 << 16), axis=0, keepdims=True) & 15
    last = jnp.max(jnp.where(mine, key_down, 0), axis=0, keepdims=True) & 15
    earlier = (owner_down == owner_across) & (down < lane)
    rank = jnp.max(jnp.where(earlier, 1, 0), axis=0, keepdims=True)
    slot = owner_across[0:1] * 2 + rank
    pick = lax.broadcasted_iota(jnp.int32, (8, 128), 0)
    return jnp.where(pick == 0, first, jnp.where(pick == 1, last, slot))


def kernel(
    q_ref, cache_ref, packed_ref, fresh_ref, gates_ref, chosen_ref, out_ref,
    own, r1, r2, r3, l1, l2, l3, x4, stage, slots, pk, fr, qb, gb, tile, tiles, acc, sel, table,
    tile_ss, tile_rs, pk_ss, pk_rs, own_ss, own_rs, misc_ss, misc_rs, q_ss, q_rs,
    ring_ss, ring_rs, pr_ss, pr_rs, x_ss, x_rs, table_sem,
):
    s = lax.axis_index("segment")
    part = lax.axis_index("seq")
    z = lax.div(part, ROW)
    col = lax.rem(part, ROW)
    x = lax.div(col, C)
    c = lax.rem(col, C)
    after = lax.rem(s + 1, SECTIONS)
    before = lax.rem(s + SECTIONS - 1, SECTIONS)

    def in_row(section, d):
        return (section, z * ROW + lax.rem(col + d + ROW, ROW))

    def in_ring(d):
        return (s, lax.rem(z + d + Z, Z) * ROW + col)

    def along(d):
        return (s, lax.rem(part + d + PARTS, PARTS))

    barrier = pltpu.get_barrier_semaphore()
    greeted = (
        [in_row(before, -d) for d in range(ROW)]
        + [in_row(s, d) for d in range(1, ROW)]
        + [in_ring(1), in_ring(-1)]
        + [along(-2), along(-4)]
    )
    for device in greeted:
        pl.semaphore_signal(barrier, inc=1, device_id=device, device_id_type=MESH)
    pl.semaphore_wait(barrier, len(greeted))

    pending = []

    def send(src, dst, send_sem, recv_sem, device):
        copy = pltpu.make_async_remote_copy(
            src_ref=src, dst_ref=dst, send_sem=send_sem, recv_sem=recv_sem,
            device_id=device, device_id_type=MESH,
        )
        copy.start()
        pending.append(copy)

    def arrived(ref, recv_sem):
        pltpu.make_async_remote_copy(
            src_ref=ref, dst_ref=ref, send_sem=recv_sem, recv_sem=recv_sem,
            device_id=in_ring(1), device_id_type=MESH,
        ).wait_recv()

    def half(ref, h):
        return ref.at[pl.ds(8 * h, 8)]

    straight = (after, part)
    for d in range(X):
        to_x = lax.rem(x + d, X)
        send(packed_ref, pk.at[:, c, z, x], pk_ss.at[d], pk_rs.at[x], (after, z * ROW + to_x * C + c))
    for h in range(2):
        send(half(cache_ref, h), half(own, h), own_ss.at[h], own_rs.at[h], straight)
    tile[...] = request_tile(chosen_ref[...])
    for d in range(ROW):
        send(tile, tiles.at[col], tile_ss.at[d], tile_rs.at[col], in_row(after, d))
    send(fresh_ref, fr.at[REACH], misc_ss.at[0], misc_rs.at[0], straight)
    send(gates_ref, gb, misc_ss.at[1], misc_rs.at[1], straight)

    def send_queries(i):
        send(q_ref.at[:, pl.ds(1024 * i, 1024)], qb.at[i], q_ss.at[i], q_rs.at[i], straight)

    right = [own, r1, r2, r3, x4]
    left = [own, l1, l2, l3, x4]

    def ring_send(k, h):
        if k < 4 or h == 0:
            send(half(right[k - 1], h), half(right[k], h), ring_ss.at[0, k - 1, h], ring_rs.at[0, k - 1, h], in_ring(1))
        if k < 4 or h == 1:
            send(half(left[k - 1], h), half(left[k], h), ring_ss.at[1, k - 1, h], ring_rs.at[1, k - 1, h], in_ring(-1))

    def ring_arrived(k, h):
        if k < 4 or h == 0:
            arrived(half(right[k], h), ring_rs.at[0, k - 1, h])
        if k < 4 or h == 1:
            arrived(half(left[k], h), ring_rs.at[1, k - 1, h])

    def packed_at(d, whole, g):
        at = lax.rem(z + d + Z, Z)
        return pk.at[:, c, at] if whole else pk.at[g, c, at]

    def packed_send(k):
        for way, sign in ((0, 1), (1, -1)):
            ref = packed_at(-sign * (k - 1), k < 4, way)
            send(ref, ref, pr_ss.at[way, k - 1], pr_rs.at[way, k - 1], in_ring(sign))

    def packed_arrived(k):
        for way, sign in ((0, 1), (1, -1)):
            arrived(packed_at(-sign * k, k < 4, way), pr_rs.at[way, k - 1])

    def serve(step, shard, d):
        owner = lax.rem(z + d + Z, Z) * ROW + col
        for e in range(ROW):
            peer = lax.rem(col + e, ROW)
            for r in range(2):
                block = shard[table[peer, r, owner]]
                if e == 0:
                    slots[owner, r] = block
                else:
                    stage[step, e - 1, r] = block
            if e > 0:
                send(stage.at[step, e - 1], slots.at[owner], x_ss.at[step, e], x_rs.at[step, e], in_row(s, e))

    def served(step, d):
        at = lax.rem(z + d + Z, Z)
        for e in range(1, ROW):
            peer = lax.rem(col - e + ROW, ROW)
            arrived(slots.at[at * ROW + peer], x_rs.at[step, e])

    def gate(branch, head, rows):
        logits = gb[rows, :].astype(jnp.float32)
        lane = lax.broadcasted_iota(jnp.int32, logits.shape, 1)
        picked = jnp.sum(jnp.where(lane == branch * 32 + head, logits, 0.0), axis=1, keepdims=True)
        return 1.0 / (1.0 + jnp.exp(-picked))

    def early_unit(i, u):
        g = i // 2
        q = jnp.concatenate(
            [qb[i, :, pl.ds(pl.multiple_of((2 * u + m) * HEAD, HEAD), HEAD)] for m in range(2)], axis=0
        )
        kv = pk[g].reshape(C * Z * X * 16, 2 * HEAD)
        scores = dot_nt(q, kv[:, :HEAD])
        peak = jnp.max(scores, axis=1, keepdims=True)
        weights = jnp.exp2((scores - peak) * EXP_SCALE).astype(jnp.bfloat16)
        mixed = dot_nn(weights, with_ones(kv[:, HEAD:]))
        summary = mixed[:, :HEAD] / mixed[:, HEAD:]

        near = fr[:, :, pl.ds(g * 2 * HEAD, 2 * HEAD)].reshape((REACH + 1) * TOKENS, 2 * HEAD)
        scores = dot_nt(q, near[:, :HEAD])
        key = lax.broadcasted_iota(jnp.int32, (2 * TOKENS, TOKENS), 1)
        token = lax.broadcasted_iota(jnp.int32, (2 * TOKENS, TOKENS), 0) & (TOKENS - 1)
        beyond = key > token
        piece = [scores[:, TOKENS * n : TOKENS * (n + 1)] for n in range(REACH + 1)]
        for n in range(REACH):
            piece[n] = jnp.where(key >= (REACH - n - part) * 1024, piece[n], MASKED)
        piece[0] = jnp.where(beyond, piece[0], piece[REACH])
        joined = jnp.concatenate(piece[:REACH], axis=1)
        peak = jnp.max(joined, axis=1, keepdims=True)
        weights = jnp.exp2((joined - peak) * EXP_SCALE)
        first = weights[:, :TOKENS]
        weights = jnp.concatenate(
            [jnp.where(beyond, first, 0.0), weights[:, TOKENS:], jnp.where(beyond, 0.0, first)], axis=1
        ).astype(jnp.bfloat16)
        mixed = dot_nn(weights, with_ones(near[:, HEAD:]))
        local = mixed[:, :HEAD] / mixed[:, HEAD:]

        for m in range(2):
            head = 8 * i + 2 * u + m
            rows = slice(TOKENS * m, TOKENS * (m + 1))
            everyone = slice(0, TOKENS)
            acc[8 * i + 2 * u + m] = (
                gate(0, head, everyone) * summary[rows] + gate(2, head, everyone) * local[rows]
            )

    def early(i):
        def body(u, carry):
            early_unit(i, u)
            return carry

        lax.fori_loop(0, 4, body, 0)

    def late_unit(b, g, u):
        rows = slice(SPAN * b, SPAN * (b + 1))
        heads = [16 * g + 4 * u + m for m in range(4)]
        q = jnp.concatenate(
            [qb[h // 8, rows, (h % 8) * HEAD : (h % 8 + 1) * HEAD] for h in heads], axis=0
        )
        kv = sel[2 * b + g]
        scores = dot_nt(q, kv[:, :HEAD])
        peak = jnp.max(scores, axis=1, keepdims=True)
        weights = jnp.exp2((scores - peak) * EXP_SCALE).astype(jnp.bfloat16)
        mixed = dot_nn(weights, with_ones(kv[:, HEAD:]))
        picked = mixed[:, :HEAD] / mixed[:, HEAD:]
        for m, h in enumerate(heads):
            one = picked[SPAN * m : SPAN * (m + 1)]
            out_ref[rows, h * HEAD : (h + 1) * HEAD] = (
                acc[h, rows, :] + gate(1, h, rows) * one
            ).astype(jnp.bfloat16)

    for d in range(X):
        arrived(pk.at[:, c, z, d], pk_rs.at[d])
    packed_send(1)
    arrived(half(own, 0), own_rs.at[0])
    ring_send(1, 0)
    packed_arrived(1)
    packed_send(2)
    arrived(half(own, 1), own_rs.at[1])
    ring_send(1, 1)
    send_queries(0)
    send_queries(1)
    for d in range(ROW):
        arrived(tiles.at[d], tile_rs.at[d])
    to_scalar = pltpu.make_async_copy(tiles, table, table_sem)
    to_scalar.start()
    to_scalar.wait()
    serve(0, own, 0)
    packed_arrived(2)
    packed_send(3)
    arrived(fr.at[REACH], misc_rs.at[0])
    send(fr.at[REACH], fr.at[2], misc_ss.at[2], misc_rs.at[2], along(2))
    send(fr.at[REACH], fr.at[0], misc_ss.at[3], misc_rs.at[3], along(4))
    ring_arrived(1, 0)
    ring_send(2, 0)
    packed_arrived(3)
    packed_send(4)
    send_queries(2)
    send_queries(3)
    ring_arrived(1, 1)
    ring_send(2, 1)
    serve(1, r1, -1)
    serve(2, l1, 1)
    packed_arrived(4)
    sibling = (s, part + 1 - 2 * c)
    send(pk.at[:, c], pk.at[:, c], misc_ss.at[4], misc_rs.at[4], sibling)
    arrived(fr.at[2], misc_rs.at[2])
    arrived(fr.at[0], misc_rs.at[3])
    send(fr.at[4 - 2 * c], fr.at[3], misc_ss.at[5], misc_rs.at[5], sibling)
    send(fr.at[2 - 2 * c], fr.at[1], misc_ss.at[6], misc_rs.at[6], sibling)
    ring_arrived(2, 0)
    ring_send(3, 0)
    arrived(pk.at[:, 1 - c], misc_rs.at[4])
    arrived(fr.at[3], misc_rs.at[5])
    arrived(fr.at[1], misc_rs.at[6])
    arrived(gb, misc_rs.at[1])
    arrived(qb.at[0], q_rs.at[0])
    early(0)
    ring_arrived(2, 1)
    ring_send(3, 1)
    serve(3, r2, -2)
    serve(4, l2, 2)
    arrived(qb.at[1], q_rs.at[1])
    early(1)
    ring_arrived(3, 0)
    ring_send(4, 0)
    arrived(qb.at[2], q_rs.at[2])
    early(2)
    ring_arrived(3, 1)
    ring_send(4, 1)
    serve(5, r3, -3)
    serve(6, l3, 3)
    arrived(qb.at[3], q_rs.at[3])
    early(3)
    ring_arrived(4, 0)
    ring_arrived(4, 1)
    serve(7, x4, 4)
    for step, d in enumerate((0, -1, 1, -2, 2, -3, 3, 4)):
        served(step, d)
    for e in range(KV_HEADS * 2 * PICKED):
        spot = table[col, 2, e]
        sel[e // PICKED, pl.ds((e % PICKED) * SPAN, SPAN), :] = slots[lax.div(spot, 2), lax.rem(spot, 2)]
    for b in range(2):
        for g in range(KV_HEADS):
            for u in range(4):
                late_unit(b, g, u)
    for copy in pending:
        copy.wait_send()


def per_device(queries, cache, packed, fresh, gates, chosen):
    q = queries[0]
    blocks = cache[0].reshape(KV_HEADS * 8, SPAN, 2 * HEAD)
    near = fresh[0].reshape(TOKENS, KV_HEADS * 2 * HEAD)
    wanted = jnp.pad(chosen[0].reshape(1, 64), ((0, 0), (0, 64)), constant_values=1 << 12)
    bf16, dma = jnp.bfloat16, pltpu.SemaphoreType.DMA
    shard = pltpu.VMEM((16, SPAN, 2 * HEAD), bf16)
    anywhere = pl.BlockSpec(memory_space=pl.ANY)
    vmem = pl.BlockSpec(memory_space=pltpu.VMEM)
    out = pl.pallas_call(
        kernel,
        out_shape=jax.ShapeDtypeStruct((TOKENS, WIDE), bf16),
        in_specs=[anywhere, anywhere, anywhere, anywhere, anywhere, vmem],
        out_specs=vmem,
        scratch_shapes=[shard] * 8
        + [
            pltpu.VMEM((8, ROW - 1, 2, SPAN, 2 * HEAD), bf16),
            pltpu.VMEM((PARTS, 2, SPAN, 2 * HEAD), bf16),
            pltpu.VMEM((KV_HEADS, C, Z, X, 16, 2 * HEAD), bf16),
            pltpu.VMEM((REACH + 1, TOKENS, KV_HEADS * 2 * HEAD), bf16),
            pltpu.VMEM((4, TOKENS, 1024), bf16),
            pltpu.VMEM((TOKENS, 96), bf16),
            pltpu.VMEM((8, 128), jnp.int32),
            pltpu.VMEM((ROW, 8, 128), jnp.int32),
            pltpu.VMEM((32, TOKENS, HEAD), jnp.float32),
            pltpu.VMEM((4, PICKED * SPAN, 2 * HEAD), bf16),
            pltpu.SMEM((ROW, 8, 128), jnp.int32),
            dma((ROW,)), dma((ROW,)),
            dma((X,)), dma((X,)),
            dma((2,)), dma((2,)),
            dma((7,)), dma((7,)),
            dma((4,)), dma((4,)),
            dma((2, 4, 2)), dma((2, 4, 2)),
            dma((2, 4)), dma((2, 4)),
            dma((8, ROW)), dma((8, ROW)),
            dma,
        ],
        compiler_params=pltpu.CompilerParams(
            collective_id=1, has_side_effects=True, vmem_limit_bytes=56 * 2**20
        ),
    )(q, blocks, packed[0], near, gates[0], wanted)
    return out[None]


def solution(mesh):
    placed = (
        P("segment", "seq", None),
        P("segment", None, "seq", None),
        P("segment", None, "seq", None),
        P("segment", "seq", None, None),
        P("segment", "seq", None),
        P("segment", "seq", None, None),
    )
    return jax.shard_map(
        per_device, mesh=mesh, in_specs=placed, out_specs=P("segment", "seq", None), check_vma=False
    )
```

time: 372 us -> 101 us (0.27)
  the two profiles are of different devices: /device:TPU:32 before, /device:TPU:1 now
where the time goes in v1:
time: 101 us
  Pallas kernels  94.3 us (93%)
  local copies, waits for them, and re-layouts  6.66 us (7%)
    pallas_call x1, Pallas kernels, per_device(): pl.pallas_call(kernel, out_shape=jax.ShapeDtypeStruct((TOKENS, WIDE), bf1...  94.3 us
    unnamed x5, local copies, waits for them, and re-layouts  6 us

profile of v1, /device:TPU:1, one launch (start us, length us, event | category | flops | bytes accessed | tf_op | source)
XLA Modules:
  0.0 100.9 jit_solution(12669677595926223011)
XLA Ops:
  0.0 0.0 copy-start
  0.0 0.7 copy-done
  0.7 0.1 reshape_squeeze.11
  0.8 0.6 pad.4.chosen_ref
  1.3 1.5 %copy.7 = bf16[1,128,96]{2,1,0:T(8,128)(2,1)} copy(bf16[1,128,96]{1,2,0:T(8,128)(2,1)} %param.10) | data formatting | bytes 49152 | tf_op args[4]
  2.8 1.6 %copy.8 = bf16[16,8,2,256]{3,1,2,0:T(8,128)(2,1)} copy(bf16[16,8,2,256]{3,2,1,0:T(2,128)(2,1)} %bitcast.13) | data formatting | bytes 262144
  4.4 94.3 %shard_map.64 = bf16[128,4096]{1,0:T(8,128)(2,1)} custom-call(bf16[128,4096]{1,0:T(8,128)(2,1)} %bitcast.9, bf16[16,64,256]{2,1,0:T(8,128)(2,1)} %bitcast.11, bf16[2,16,256]{2,1,0:T(8,128)(2,1)} %bitcast.14, bf16[128,512]{1,0:T(8,128)(2,1)} %bitcast.10, bf16[128,96]{1,0:T(8,128)(2,1)} %bitcast.12, s32[1,128]{1,0:T(1,128)} %pad.4.chosen_ref), custom_call_target="tpu_custom_call" | custom-call | tf_op jit(solution)/shard_map/pallas_call | solution.py:333
  98.6 2.3 %copy.10 = bf16[1,128,4096]{2,1,0:T(8,128)(2,1)} copy(bf16[1,128,4096]{2,1,0:T(8,128)(2,1)} %bitcast.8) | data formatting | bytes 2097152
Async XLA Ops:
  0.0 0.7 copy-start

commit v2 on v1

--- a/solution.py
+++ b/solution.py
@@ -19,6 +19,8 @@
 PARTS = Z * ROW
 SECTIONS = 4
 REACH = 4
+CHUNKS = 4
+PIECE = KV_HEADS * 8 // CHUNKS
 MESH = pl.DeviceIdType.MESH
 MASKED = -1e30
 EXP_SCALE = HEAD**-0.5 * 1.4426950408889634
@@ -56,11 +58,26 @@
     return jnp.where(pick == 0, first, jnp.where(pick == 1, last, slot))
 
 
+def chosen_row(chosen_ref, listed):
+    listed[...] = jnp.zeros(listed.shape, listed.dtype)
+    for b in range(2):
+        listed[KV_HEADS * b : KV_HEADS * (b + 1), 0:PICKED] = chosen_ref[b]
+    lane = lax.broadcasted_iota(jnp.int32, (1, 128), 1)
+    row = jnp.full((1, 128), 1 << 12, jnp.int32)
+    for i in range(2 * KV_HEADS):
+        part = listed[i : i + 1, :]
+        if i > 0:
+            part = pltpu.roll(part, PICKED * i, 1)
+        row = jnp.where((lane >= PICKED * i) & (lane < PICKED * (i + 1)), part, row)
+    return row
+
+
 def kernel(
     q_ref, cache_ref, packed_ref, fresh_ref, gates_ref, chosen_ref, out_ref,
-    own, r1, r2, r3, l1, l2, l3, x4, stage, slots, pk, fr, qb, gb, tile, tiles, acc, sel, table,
+    own, r1, r2, r3, l1, l2, l3, x4, stage, slots, pk, raw, behind, fr, qb, gb, gate_of,
+    listed, tile, tiles, acc, sel, table,
     tile_ss, tile_rs, pk_ss, pk_rs, own_ss, own_rs, misc_ss, misc_rs, q_ss, q_rs,
-    ring_ss, ring_rs, pr_ss, pr_rs, x_ss, x_rs, table_sem,
+    ring_ss, ring_rs, pr_ss, pr_rs, x_ss, x_rs, local_sem,
 ):
     s = lax.axis_index("segment")
     part = lax.axis_index("seq")
@@ -101,44 +118,43 @@
         copy.start()
         pending.append(copy)
 
+    others = ((1, 0), (3, 0), (1, 1), (3, 1), (2, 0), (2, 1), (0, 1))
+
+    def there(dx, dc):
+        return lax.rem(x + dx + X, X) * C + lax.rem(c + dc, C)
+
     def arrived(ref, recv_sem):
         pltpu.make_async_remote_copy(
             src_ref=ref, dst_ref=ref, send_sem=recv_sem, recv_sem=recv_sem,
             device_id=in_ring(1), device_id_type=MESH,
         ).wait_recv()
 
-    def half(ref, h):
-        return ref.at[pl.ds(8 * h, 8)]
+    def piece_of(ref, i):
+        return ref.at[pl.ds(PIECE * i, PIECE)]
 
     straight = (after, part)
-    for d in range(X):
-        to_x = lax.rem(x + d, X)
-        send(packed_ref, pk.at[:, c, z, x], pk_ss.at[d], pk_rs.at[x], (after, z * ROW + to_x * C + c))
-    for h in range(2):
-        send(half(cache_ref, h), half(own, h), own_ss.at[h], own_rs.at[h], straight)
-    tile[...] = request_tile(chosen_ref[...])
-    for d in range(ROW):
-        send(tile, tiles.at[col], tile_ss.at[d], tile_rs.at[col], in_row(after, d))
-    send(fresh_ref, fr.at[REACH], misc_ss.at[0], misc_rs.at[0], straight)
-    send(gates_ref, gb, misc_ss.at[1], misc_rs.at[1], straight)
+
+    def send_cache(i):
+        send(piece_of(cache_ref, i), piece_of(own, i), own_ss.at[i], own_rs.at[i], straight)
 
     def send_queries(i):
         send(q_ref.at[:, pl.ds(1024 * i, 1024)], qb.at[i], q_ss.at[i], q_rs.at[i], straight)
 
+    def ring_send(k, i):
+        for way, (held, sign) in enumerate(((right, 1), (left, -1))):
+            if k < 4 or i // (CHUNKS // 2) == way:
+                send(
+                    piece_of(held[k - 1], i), piece_of(held[k], i),
+                    ring_ss.at[way, k - 1, i], ring_rs.at[way, k - 1, i], in_ring(sign),
+                )
+
+    def ring_arrived(k, i):
+        for way, held in enumerate((right, left)):
+            if k < 4 or i // (CHUNKS // 2) == way:
+                arrived(piece_of(held[k], i), ring_rs.at[way, k - 1, i])
+
     right = [own, r1, r2, r3, x4]
     left = [own, l1, l2, l3, x4]
-
-    def ring_send(k, h):
-        if k < 4 or h == 0:
-            send(half(right[k - 1], h), half(right[k], h), ring_ss.at[0, k - 1, h], ring_rs.at[0, k - 1, h], in_ring(1))
-        if k < 4 or h == 1:
-            send(half(left[k - 1], h), half(left[k], h), ring_ss.at[1, k - 1, h], ring_rs.at[1, k - 1, h], in_ring(-1))
-
-    def ring_arrived(k, h):
-        if k < 4 or h == 0:
-            arrived(half(right[k], h), ring_rs.at[0, k - 1, h])
-        if k < 4 or h == 1:
-            arrived(half(left[k], h), ring_rs.at[1, k - 1, h])
 
     def packed_at(d, whole, g):
         at = lax.rem(z + d + Z, Z)
@@ -155,28 +171,26 @@
 
     def serve(step, shard, d):
         owner = lax.rem(z + d + Z, Z) * ROW + col
-        for e in range(ROW):
-            peer = lax.rem(col + e, ROW)
+        for e, (dx, dc) in enumerate(others + ((0, 0),)):
+            peer = there(dx, dc)
             for r in range(2):
                 block = shard[table[peer, r, owner]]
-                if e == 0:
+                if e == ROW - 1:
                     slots[owner, r] = block
                 else:
-                    stage[step, e - 1, r] = block
-            if e > 0:
-                send(stage.at[step, e - 1], slots.at[owner], x_ss.at[step, e], x_rs.at[step, e], in_row(s, e))
+                    stage[step, e, r] = block
+            if e < ROW - 1:
+                send(stage.at[step, e], slots.at[owner], x_ss.at[step, e], x_rs.at[step, e], (s, z * ROW + peer))
 
     def served(step, d):
         at = lax.rem(z + d + Z, Z)
-        for e in range(1, ROW):
-            peer = lax.rem(col - e + ROW, ROW)
-            arrived(slots.at[at * ROW + peer], x_rs.at[step, e])
+        for e, (dx, dc) in enumerate(others):
+            arrived(slots.at[at * ROW + there(-dx, dc)], x_rs.at[step, e])
 
     def gate(branch, head, rows):
-        logits = gb[rows, :].astype(jnp.float32)
-        lane = lax.broadcasted_iota(jnp.int32, logits.shape, 1)
-        picked = jnp.sum(jnp.where(lane == branch * 32 + head, logits, 0.0), axis=1, keepdims=True)
-        return 1.0 / (1.0 + jnp.exp(-picked))
+        values = gate_of[rows, :]
+        lane = lax.broadcasted_iota(jnp.int32, values.shape, 1)
+        return jnp.sum(jnp.where(lane == branch * 32 + head, values, 0.0), axis=1, keepdims=True)
 
     def early_unit(i, u):
         g = i // 2
@@ -217,12 +231,12 @@
                 gate(0, head, everyone) * summary[rows] + gate(2, head, everyone) * local[rows]
             )
 
-    def early(i):
+    def early(i, half):
         def body(u, carry):
             early_unit(i, u)
             return carry
 
-        lax.fori_loop(0, 4, body, 0)
+        lax.fori_loop(2 * half, 2 * half + 2, body, 0)
 
     def late_unit(b, g, u):
         rows = slice(SPAN * b, SPAN * (b + 1))
@@ -242,72 +256,98 @@
                 acc[h, rows, :] + gate(1, h, rows) * one
             ).astype(jnp.bfloat16)
 
+    send_cache(0)
     for d in range(X):
-        arrived(pk.at[:, c, z, d], pk_rs.at[d])
-    packed_send(1)
-    arrived(half(own, 0), own_rs.at[0])
-    ring_send(1, 0)
-    packed_arrived(1)
-    packed_send(2)
-    arrived(half(own, 1), own_rs.at[1])
-    ring_send(1, 1)
-    send_queries(0)
-    send_queries(1)
+        to_x = lax.rem(x + d, X)
+        send(packed_ref, pk.at[:, c, z, x], pk_ss.at[d], pk_rs.at[x], (after, z * ROW + to_x * C + c))
+    send_cache(1)
+    fetch = pltpu.make_async_copy(fresh_ref, raw, local_sem.at[0])
+    fetch.start()
+    tile[...] = request_tile(chosen_row(chosen_ref, listed))
+    for d in range(ROW):
+        send(tile, tiles.at[col], tile_ss.at[d], tile_rs.at[col], in_row(after, d))
+    send(gates_ref, gb, misc_ss.at[1], misc_rs.at[1], straight)
+    fetch.wait()
+    for g in range(KV_HEADS):
+        behind[0, :, 2 * HEAD * g : 2 * HEAD * (g + 1)] = raw[:, g, :]
+    send(behind.at[0], behind.at[1], misc_ss.at[2], misc_rs.at[2], along(2))
+    send(behind.at[0], behind.at[2], misc_ss.at[3], misc_rs.at[3], along(4))
+    sibling = (s, part + 1 - 2 * c)
+
+    for i in range(CHUNKS):
+        arrived(piece_of(own, i), own_rs.at[i])
+        ring_send(1, i)
+        if i + 2 < CHUNKS:
+            send_cache(i + 2)
+        if i == 0:
+            for d in range(X):
+                arrived(pk.at[:, c, z, d], pk_rs.at[d])
+            packed_send(1)
+        if i == 2:
+            packed_arrived(1)
+            packed_send(2)
     for d in range(ROW):
         arrived(tiles.at[d], tile_rs.at[d])
-    to_scalar = pltpu.make_async_copy(tiles, table, table_sem)
+    to_scalar = pltpu.make_async_copy(tiles, table, local_sem.at[1])
     to_scalar.start()
     to_scalar.wait()
     serve(0, own, 0)
-    packed_arrived(2)
-    packed_send(3)
-    arrived(fr.at[REACH], misc_rs.at[0])
-    send(fr.at[REACH], fr.at[2], misc_ss.at[2], misc_rs.at[2], along(2))
-    send(fr.at[REACH], fr.at[0], misc_ss.at[3], misc_rs.at[3], along(4))
-    ring_arrived(1, 0)
-    ring_send(2, 0)
-    packed_arrived(3)
-    packed_send(4)
-    send_queries(2)
-    send_queries(3)
-    ring_arrived(1, 1)
-    ring_send(2, 1)
+    arrived(behind.at[1], misc_rs.at[2])
+    arrived(behind.at[2], misc_rs.at[3])
+    for n, spot in enumerate((4, 2, 0)):
+        send(behind.at[n], fr.at[spot], misc_ss.at[7 + n], misc_rs.at[7 + n], straight)
+    for i in range(CHUNKS):
+        ring_arrived(1, i)
+        ring_send(2, i)
+        if i == 0:
+            packed_arrived(2)
+            packed_send(3)
+        if i == 2:
+            packed_arrived(3)
+            packed_send(4)
+    send_queries(0)
+    send_queries(1)
     serve(1, r1, -1)
     serve(2, l1, 1)
-    packed_arrived(4)
-    sibling = (s, part + 1 - 2 * c)
-    send(pk.at[:, c], pk.at[:, c], misc_ss.at[4], misc_rs.at[4], sibling)
-    arrived(fr.at[2], misc_rs.at[2])
-    arrived(fr.at[0], misc_rs.at[3])
-    send(fr.at[4 - 2 * c], fr.at[3], misc_ss.at[5], misc_rs.at[5], sibling)
-    send(fr.at[2 - 2 * c], fr.at[1], misc_ss.at[6], misc_rs.at[6], sibling)
-    ring_arrived(2, 0)
-    ring_send(3, 0)
+    for i in range(CHUNKS):
+        ring_arrived(2, i)
+        ring_send(3, i)
+        if i == 0:
+            packed_arrived(4)
+            send(pk.at[:, c], pk.at[:, c], misc_ss.at[4], misc_rs.at[4], sibling)
+        if i == 1:
+            for n, spot in enumerate((4, 2, 0)):
+                arrived(fr.at[spot], misc_rs.at[7 + n])
+            send(fr.at[4 - 2 * c], fr.at[3], misc_ss.at[5], misc_rs.at[5], sibling)
+            send(fr.at[2 - 2 * c], fr.at[1], misc_ss.at[6], misc_rs.at[6], sibling)
+    serve(3, r2, -2)
+    serve(4, l2, 2)
+    arrived(gb, misc_rs.at[1])
+    logits = jnp.concatenate([gb[...].astype(jnp.float32), jnp.zeros((32, TOKENS), jnp.float32)], axis=0)
+    gate_of[...] = 1.0 / (1.0 + jnp.exp(-logits.T))
     arrived(pk.at[:, 1 - c], misc_rs.at[4])
     arrived(fr.at[3], misc_rs.at[5])
     arrived(fr.at[1], misc_rs.at[6])
-    arrived(gb, misc_rs.at[1])
     arrived(qb.at[0], q_rs.at[0])
-    early(0)
-    ring_arrived(2, 1)
-    ring_send(3, 1)
-    serve(3, r2, -2)
-    serve(4, l2, 2)
-    arrived(qb.at[1], q_rs.at[1])
-    early(1)
-    ring_arrived(3, 0)
-    ring_send(4, 0)
-    arrived(qb.at[2], q_rs.at[2])
-    early(2)
-    ring_arrived(3, 1)
-    ring_send(4, 1)
+    send_queries(2)
+    for i in range(CHUNKS):
+        ring_arrived(3, i)
+        ring_send(4, i)
+        if i == 2:
+            arrived(qb.at[1], q_rs.at[1])
+            send_queries(3)
+        if i < 3:
+            early(i // 2, i % 2)
     serve(5, r3, -3)
     serve(6, l3, 3)
-    arrived(qb.at[3], q_rs.at[3])
-    early(3)
-    ring_arrived(4, 0)
-    ring_arrived(4, 1)
+    early(1, 1)
+    for i in range(CHUNKS):
+        ring_arrived(4, i)
     serve(7, x4, 4)
+    for i in (2, 3):
+        arrived(qb.at[i], q_rs.at[i])
+        early(i, 0)
+        early(i, 1)
     for step, d in enumerate((0, -1, 1, -2, 2, -3, 3, 4)):
         served(step, d)
     for e in range(KV_HEADS * 2 * PICKED):
@@ -322,13 +362,10 @@
 
 
 def per_device(queries, cache, packed, fresh, gates, chosen):
-    q = queries[0]
     blocks = cache[0].reshape(KV_HEADS * 8, SPAN, 2 * HEAD)
-    near = fresh[0].reshape(TOKENS, KV_HEADS * 2 * HEAD)
-    wanted = jnp.pad(chosen[0].reshape(1, 64), ((0, 0), (0, 64)), constant_values=1 << 12)
     bf16, dma = jnp.bfloat16, pltpu.SemaphoreType.DMA
     shard = pltpu.VMEM((16, SPAN, 2 * HEAD), bf16)
-    anywhere = pl.BlockSpec(memory_space=pl.ANY)
+    anywhere = pl.BlockSpec(memory_space=pltpu.HBM)
     vmem = pl.BlockSpec(memory_space=pltpu.VMEM)
     out = pl.pallas_call(
         kernel,
@@ -340,9 +377,13 @@
             pltpu.VMEM((8, ROW - 1, 2, SPAN, 2 * HEAD), bf16),
             pltpu.VMEM((PARTS, 2, SPAN, 2 * HEAD), bf16),
             pltpu.VMEM((KV_HEADS, C, Z, X, 16, 2 * HEAD), bf16),
+            pltpu.VMEM((TOKENS, KV_HEADS, 2 * HEAD), bf16),
+            pltpu.VMEM((3, TOKENS, KV_HEADS * 2 * HEAD), bf16),
             pltpu.VMEM((REACH + 1, TOKENS, KV_HEADS * 2 * HEAD), bf16),
             pltpu.VMEM((4, TOKENS, 1024), bf16),
-            pltpu.VMEM((TOKENS, 96), bf16),
+            pltpu.VMEM((96, TOKENS), bf16),
+            pltpu.VMEM((TOKENS, 128), jnp.float32),
+            pltpu.VMEM((8, 128), jnp.int32),
             pltpu.VMEM((8, 128), jnp.int32),
             pltpu.VMEM((ROW, 8, 128), jnp.int32),
             pltpu.VMEM((32, TOKENS, HEAD), jnp.float32),
@@ -350,18 +391,18 @@
             pltpu.SMEM((ROW, 8, 128), jnp.int32),
             dma((ROW,)), dma((ROW,)),
             dma((X,)), dma((X,)),
-            dma((2,)), dma((2,)),
-            dma((7,)), dma((7,)),
+            dma((CHUNKS,)), dma((CHUNKS,)),
+            dma((10,)), dma((10,)),
             dma((4,)), dma((4,)),
-            dma((2, 4, 2)), dma((2, 4, 2)),
+            dma((2, 4, CHUNKS)), dma((2, 4, CHUNKS)),
             dma((2, 4)), dma((2, 4)),
             dma((8, ROW)), dma((8, ROW)),
-            dma,
+            dma((2,)),
         ],
         compiler_params=pltpu.CompilerParams(
             collective_id=1, has_side_effects=True, vmem_limit_bytes=56 * 2**20
         ),
-    )(q, blocks, packed[0], near, gates[0], wanted)
+    )(queries[0], blocks, packed[0], fresh[0], gates[0].T, chosen[0])
     return out[None]
 
 

time: 101 us -> 89.9 us (0.89)
  Pallas kernels: 94.3 us -> 87.4 us
  local copies, waits for them, and re-layouts: 6.66 us -> 2.29 us
    pallas_call x1, Pallas kernels: 94.3 us -> 87.4 us  [per_device(): pl.pallas_call(kernel, out_shape=jax.ShapeDtypeStruct((TOKENS, WIDE), bf1...]
    unnamed x5 -> x1, local copies, waits for them, and re-layouts: 6 us -> 2.29 us
where the time goes in v2:
time: 89.9 us; the launch traced here: 89.7 us
  Pallas kernels  87.4 us (97%)
  local copies, waits for them, and re-layouts  2.29 us (3%)
    pallas_call x1, Pallas kernels, per_device(): pl.pallas_call(kernel, out_shape=jax.ShapeDtypeStruct((TOKENS, WIDE), bf1...  87.4 us
    unnamed x1, local copies, waits for them, and re-layouts  2.29 us

profile of v2, /device:TPU:1, one launch (start us, length us, event | category | flops | bytes accessed | tf_op | source)
XLA Modules:
  0.0 89.7 jit_solution(17437813220998361685)
XLA Ops:
  0.0 87.4 %shard_map.64 = bf16[128,4096]{1,0:T(8,128)(2,1)} custom-call(bf16[128,4096]{1,0:T(8,128)(2,1)} %bitcast.10, bf16[16,64,256]{2,1,0:T(8,128)(2,1)} %bitcast.11, bf16[2,16,256]{2,1,0:T(8,128)(2,1)} %bitcast.14, bf16[128,2,256]{2,1,0:T(2,128)(2,1)} %bitcast.12, bf16[96,128]{1,0:T(8,128)(2,1)} %bitcast.13, s32[2,2,16]{2,1,0:T(2,128)} %bitcast.15), custom_call_target="tpu_custom_call" | custom-call | tf_op jit(solution)/shard_map/pallas_call | solution.py:370
  87.4 2.3 %copy.8 = bf16[1,128,4096]{2,1,0:T(8,128)(2,1)} copy(bf16[1,128,4096]{2,1,0:T(8,128)(2,1)} %bitcast.9) | data formatting | bytes 2097152

commit v3 on v2

--- a/solution.py
+++ b/solution.py
@@ -74,10 +74,10 @@
 
 def kernel(
     q_ref, cache_ref, packed_ref, fresh_ref, gates_ref, chosen_ref, out_ref,
-    own, r1, r2, r3, l1, l2, l3, x4, stage, slots, pk, raw, behind, fr, qb, gb, gate_of,
-    listed, tile, tiles, acc, sel, table,
+    own, r1, r2, r3, l1, l2, l3, x4, stage, slots, home_pk, pk, raw, behind, fr, qb, gb,
+    gate_of, chosen, listed, tile, tiles, acc, sel, table,
     tile_ss, tile_rs, pk_ss, pk_rs, own_ss, own_rs, misc_ss, misc_rs, q_ss, q_rs,
-    ring_ss, ring_rs, pr_ss, pr_rs, x_ss, x_rs, local_sem,
+    ring_ss, ring_rs, x_ss, x_rs, local_sem,
 ):
     s = lax.axis_index("segment")
     part = lax.axis_index("seq")
@@ -101,11 +101,17 @@
     greeted = (
         [in_row(before, -d) for d in range(ROW)]
         + [in_row(s, d) for d in range(1, ROW)]
-        + [in_ring(1), in_ring(-1)]
+        + [in_ring(d) for d in range(1, Z)]
         + [along(-2), along(-4)]
     )
     for device in greeted:
         pl.semaphore_signal(barrier, inc=1, device_id=device, device_id_type=MESH)
+    keep = pltpu.make_async_copy(packed_ref, home_pk.at[x, z], local_sem.at[0])
+    keep.start()
+    fetch = pltpu.make_async_copy(fresh_ref, raw, local_sem.at[1])
+    fetch.start()
+    fetch_chosen = pltpu.make_async_copy(chosen_ref, chosen, local_sem.at[3])
+    fetch_chosen.start()
     pl.semaphore_wait(barrier, len(greeted))
 
     pending = []
@@ -155,19 +161,6 @@
 
     right = [own, r1, r2, r3, x4]
     left = [own, l1, l2, l3, x4]
-
-    def packed_at(d, whole, g):
-        at = lax.rem(z + d + Z, Z)
-        return pk.at[:, c, at] if whole else pk.at[g, c, at]
-
-    def packed_send(k):
-        for way, sign in ((0, 1), (1, -1)):
-            ref = packed_at(-sign * (k - 1), k < 4, way)
-            send(ref, ref, pr_ss.at[way, k - 1], pr_rs.at[way, k - 1], in_ring(sign))
-
-    def packed_arrived(k):
-        for way, sign in ((0, 1), (1, -1)):
-            arrived(packed_at(-sign * k, k < 4, way), pr_rs.at[way, k - 1])
 
     def serve(step, shard, d):
         owner = lax.rem(z + d + Z, Z) * ROW + col
@@ -183,9 +176,9 @@
                 send(stage.at[step, e], slots.at[owner], x_ss.at[step, e], x_rs.at[step, e], (s, z * ROW + peer))
 
     def served(step, d):
-        at = lax.rem(z + d + Z, Z)
+        first = lax.rem(z + d + Z, Z) * ROW
         for e, (dx, dc) in enumerate(others):
-            arrived(slots.at[at * ROW + there(-dx, dc)], x_rs.at[step, e])
+            arrived(slots.at[first + there(-dx, dc)], x_rs.at[step, e])
 
     def gate(branch, head, rows):
         values = gate_of[rows, :]
@@ -197,7 +190,7 @@
         q = jnp.concatenate(
             [qb[i, :, pl.ds(pl.multiple_of((2 * u + m) * HEAD, HEAD), HEAD)] for m in range(2)], axis=0
         )
-        kv = pk[g].reshape(C * Z * X * 16, 2 * HEAD)
+        kv = pk[:, :, :, g].reshape(C * X * Z * 16, 2 * HEAD)
         scores = dot_nt(q, kv[:, :HEAD])
         peak = jnp.max(scores, axis=1, keepdims=True)
         weights = jnp.exp2((scores - peak) * EXP_SCALE).astype(jnp.bfloat16)
@@ -256,95 +249,86 @@
                 acc[h, rows, :] + gate(1, h, rows) * one
             ).astype(jnp.bfloat16)
 
+    sibling = (s, part + 1 - 2 * c)
     send_cache(0)
-    for d in range(X):
-        to_x = lax.rem(x + d, X)
-        send(packed_ref, pk.at[:, c, z, x], pk_ss.at[d], pk_rs.at[x], (after, z * ROW + to_x * C + c))
-    send_cache(1)
-    fetch = pltpu.make_async_copy(fresh_ref, raw, local_sem.at[0])
-    fetch.start()
-    tile[...] = request_tile(chosen_row(chosen_ref, listed))
+    for d in range(1, Z):
+        send(packed_ref, home_pk.at[x, z], pk_ss.at[d], pk_rs.at[d], in_ring(d))
+    fetch_chosen.wait()
+    tile[...] = request_tile(chosen_row(chosen, listed))
     for d in range(ROW):
         send(tile, tiles.at[col], tile_ss.at[d], tile_rs.at[col], in_row(after, d))
-    send(gates_ref, gb, misc_ss.at[1], misc_rs.at[1], straight)
+    for i in range(1, CHUNKS):
+        send_cache(i)
     fetch.wait()
     for g in range(KV_HEADS):
         behind[0, :, 2 * HEAD * g : 2 * HEAD * (g + 1)] = raw[:, g, :]
     send(behind.at[0], behind.at[1], misc_ss.at[2], misc_rs.at[2], along(2))
     send(behind.at[0], behind.at[2], misc_ss.at[3], misc_rs.at[3], along(4))
-    sibling = (s, part + 1 - 2 * c)
-
     for i in range(CHUNKS):
         arrived(piece_of(own, i), own_rs.at[i])
         ring_send(1, i)
-        if i + 2 < CHUNKS:
-            send_cache(i + 2)
         if i == 0:
-            for d in range(X):
-                arrived(pk.at[:, c, z, d], pk_rs.at[d])
-            packed_send(1)
-        if i == 2:
-            packed_arrived(1)
-            packed_send(2)
-    for d in range(ROW):
-        arrived(tiles.at[d], tile_rs.at[d])
-    to_scalar = pltpu.make_async_copy(tiles, table, local_sem.at[1])
-    to_scalar.start()
+            for d in range(ROW):
+                arrived(tiles.at[d], tile_rs.at[d])
+            to_scalar = pltpu.make_async_copy(tiles, table, local_sem.at[2])
+            to_scalar.start()
+        if i == 1:
+            keep.wait()
+            for d in range(1, Z):
+                arrived(home_pk.at[x, lax.rem(z - d + Z, Z)], pk_rs.at[d])
+            for d in range(1, X):
+                to = (s, z * ROW + lax.rem(x + d, X) * C + c)
+                send(home_pk.at[x], home_pk.at[x], pk_ss.at[Z + d], pk_rs.at[Z + d], to)
     to_scalar.wait()
     serve(0, own, 0)
+    for d in range(1, X):
+        arrived(home_pk.at[lax.rem(x - d + X, X)], pk_rs.at[Z + d])
+    send(home_pk, pk.at[c], misc_ss.at[4], misc_rs.at[4], straight)
     arrived(behind.at[1], misc_rs.at[2])
     arrived(behind.at[2], misc_rs.at[3])
     for n, spot in enumerate((4, 2, 0)):
         send(behind.at[n], fr.at[spot], misc_ss.at[7 + n], misc_rs.at[7 + n], straight)
+    send(gates_ref, gb, misc_ss.at[1], misc_rs.at[1], straight)
+    send_queries(0)
     for i in range(CHUNKS):
         ring_arrived(1, i)
         ring_send(2, i)
-        if i == 0:
-            packed_arrived(2)
-            packed_send(3)
-        if i == 2:
-            packed_arrived(3)
-            packed_send(4)
-    send_queries(0)
-    send_queries(1)
     serve(1, r1, -1)
     serve(2, l1, 1)
+    send_queries(1)
     for i in range(CHUNKS):
         ring_arrived(2, i)
         ring_send(3, i)
-        if i == 0:
-            packed_arrived(4)
-            send(pk.at[:, c], pk.at[:, c], misc_ss.at[4], misc_rs.at[4], sibling)
+    serve(3, r2, -2)
+    serve(4, l2, 2)
+    send_queries(2)
+    for i in range(CHUNKS):
+        ring_arrived(3, i)
+        ring_send(4, i)
         if i == 1:
+            arrived(pk.at[c], misc_rs.at[4])
+            send(pk.at[c], pk.at[c], misc_ss.at[10], misc_rs.at[10], sibling)
+        if i == 2:
             for n, spot in enumerate((4, 2, 0)):
                 arrived(fr.at[spot], misc_rs.at[7 + n])
             send(fr.at[4 - 2 * c], fr.at[3], misc_ss.at[5], misc_rs.at[5], sibling)
             send(fr.at[2 - 2 * c], fr.at[1], misc_ss.at[6], misc_rs.at[6], sibling)
-    serve(3, r2, -2)
-    serve(4, l2, 2)
+    serve(5, r3, -3)
+    serve(6, l3, 3)
+    send_queries(3)
     arrived(gb, misc_rs.at[1])
     logits = jnp.concatenate([gb[...].astype(jnp.float32), jnp.zeros((32, TOKENS), jnp.float32)], axis=0)
     gate_of[...] = 1.0 / (1.0 + jnp.exp(-logits.T))
-    arrived(pk.at[:, 1 - c], misc_rs.at[4])
+    arrived(pk.at[1 - c], misc_rs.at[10])
     arrived(fr.at[3], misc_rs.at[5])
     arrived(fr.at[1], misc_rs.at[6])
     arrived(qb.at[0], q_rs.at[0])
-    send_queries(2)
-    for i in range(CHUNKS):
-        ring_arrived(3, i)
-        ring_send(4, i)
-        if i == 2:
-            arrived(qb.at[1], q_rs.at[1])
-            send_queries(3)
-        if i < 3:
-            early(i // 2, i % 2)
-    serve(5, r3, -3)
-    serve(6, l3, 3)
-    early(1, 1)
+    early(0, 0)
+    early(0, 1)
     for i in range(CHUNKS):
         ring_arrived(4, i)
     serve(7, x4, 4)
-    for i in (2, 3):
+    for i in range(1, 4):
         arrived(qb.at[i], q_rs.at[i])
         early(i, 0)
         early(i, 1)
@@ -370,19 +354,21 @@
     out = pl.pallas_call(
         kernel,
         out_shape=jax.ShapeDtypeStruct((TOKENS, WIDE), bf16),
-        in_specs=[anywhere, anywhere, anywhere, anywhere, anywhere, vmem],
+        in_specs=[anywhere] * 6,
         out_specs=vmem,
         scratch_shapes=[shard] * 8
         + [
             pltpu.VMEM((8, ROW - 1, 2, SPAN, 2 * HEAD), bf16),
             pltpu.VMEM((PARTS, 2, SPAN, 2 * HEAD), bf16),
-            pltpu.VMEM((KV_HEADS, C, Z, X, 16, 2 * HEAD), bf16),
+            pltpu.VMEM((X, Z, KV_HEADS, 16, 2 * HEAD), bf16),
+            pltpu.VMEM((C, X, Z, KV_HEADS, 16, 2 * HEAD), bf16),
             pltpu.VMEM((TOKENS, KV_HEADS, 2 * HEAD), bf16),
             pltpu.VMEM((3, TOKENS, KV_HEADS * 2 * HEAD), bf16),
             pltpu.VMEM((REACH + 1, TOKENS, KV_HEADS * 2 * HEAD), bf16),
             pltpu.VMEM((4, TOKENS, 1024), bf16),
             pltpu.VMEM((96, TOKENS), bf16),
             pltpu.VMEM((TOKENS, 128), jnp.float32),
+            pltpu.VMEM((2, KV_HEADS, PICKED), jnp.int32),
             pltpu.VMEM((8, 128), jnp.int32),
             pltpu.VMEM((8, 128), jnp.int32),
             pltpu.VMEM((ROW, 8, 128), jnp.int32),
@@ -390,14 +376,13 @@
             pltpu.VMEM((4, PICKED * SPAN, 2 * HEAD), bf16),
             pltpu.SMEM((ROW, 8, 128), jnp.int32),
             dma((ROW,)), dma((ROW,)),
-            dma((X,)), dma((X,)),
+            dma((Z + X,)), dma((Z + X,)),
             dma((CHUNKS,)), dma((CHUNKS,)),
-            dma((10,)), dma((10,)),
+            dma((11,)), dma((11,)),
             dma((4,)), dma((4,)),
             dma((2, 4, CHUNKS)), dma((2, 4, CHUNKS)),
-            dma((2, 4)), dma((2, 4)),
             dma((8, ROW)), dma((8, ROW)),
-            dma((2,)),
+            dma((4,)),
         ],
         compiler_params=pltpu.CompilerParams(
             collective_id=1, has_side_effects=True, vmem_limit_bytes=56 * 2**20

time: 89.9 us -> 85.6 us (0.952)
  the two profiles are of different devices: /device:TPU:1 before, /device:TPU:32 now
where the time goes in v3:
time: 85.6 us; the launch traced here: 84.5 us
  Pallas kernels  82.2 us (96%)
  local copies, waits for them, and re-layouts  2.29 us (3%)
    pallas_call x1, Pallas kernels, per_device(): pl.pallas_call(kernel, out_shape=jax.ShapeDtypeStruct((TOKENS, WIDE), bf1...  82.2 us
    unnamed x1, local copies, waits for them, and re-layouts  2.29 us

profile of v3, /device:TPU:32, one launch (start us, length us, event | category | flops | bytes accessed | tf_op | source)
XLA Modules:
  0.0 84.5 jit_solution(17865280515177465941)
XLA Ops:
  0.0 82.2 %shard_map.64 = bf16[128,4096]{1,0:T(8,128)(2,1)} custom-call(bf16[128,4096]{1,0:T(8,128)(2,1)} %bitcast.10, bf16[16,64,256]{2,1,0:T(8,128)(2,1)} %bitcast.11, bf16[2,16,256]{2,1,0:T(8,128)(2,1)} %bitcast.14, bf16[128,2,256]{2,1,0:T(2,128)(2,1)} %bitcast.12, bf16[96,128]{1,0:T(8,128)(2,1)} %bitcast.13, s32[2,2,16]{2,1,0:T(2,128)} %bitcast.15), custom_call_target="tpu_custom_call" | custom-call | tf_op jit(solution)/shard_map/pallas_call | solution.py:354
  82.2 2.3 %copy.8 = bf16[1,128,4096]{2,1,0:T(8,128)(2,1)} copy(bf16[1,128,4096]{2,1,0:T(8,128)(2,1)} %bitcast.9) | data formatting | bytes 2097152

commit v4 on v3

--- a/solution.py
+++ b/solution.py
@@ -251,13 +251,14 @@
 
     sibling = (s, part + 1 - 2 * c)
     send_cache(0)
+    send_cache(1)
     for d in range(1, Z):
         send(packed_ref, home_pk.at[x, z], pk_ss.at[d], pk_rs.at[d], in_ring(d))
     fetch_chosen.wait()
     tile[...] = request_tile(chosen_row(chosen, listed))
     for d in range(ROW):
         send(tile, tiles.at[col], tile_ss.at[d], tile_rs.at[col], in_row(after, d))
-    for i in range(1, CHUNKS):
+    for i in range(2, CHUNKS):
         send_cache(i)
     fetch.wait()
     for g in range(KV_HEADS):
@@ -267,7 +268,7 @@
     for i in range(CHUNKS):
         arrived(piece_of(own, i), own_rs.at[i])
         ring_send(1, i)
-        if i == 0:
+        if i == 2:
             for d in range(ROW):
                 arrived(tiles.at[d], tile_rs.at[d])
             to_scalar = pltpu.make_async_copy(tiles, table, local_sem.at[2])
@@ -289,19 +290,18 @@
     for n, spot in enumerate((4, 2, 0)):
         send(behind.at[n], fr.at[spot], misc_ss.at[7 + n], misc_rs.at[7 + n], straight)
     send(gates_ref, gb, misc_ss.at[1], misc_rs.at[1], straight)
-    send_queries(0)
+    for i in range(4):
+        send_queries(i)
     for i in range(CHUNKS):
         ring_arrived(1, i)
         ring_send(2, i)
     serve(1, r1, -1)
     serve(2, l1, 1)
-    send_queries(1)
     for i in range(CHUNKS):
         ring_arrived(2, i)
         ring_send(3, i)
     serve(3, r2, -2)
     serve(4, l2, 2)
-    send_queries(2)
     for i in range(CHUNKS):
         ring_arrived(3, i)
         ring_send(4, i)
@@ -315,7 +315,6 @@
             send(fr.at[2 - 2 * c], fr.at[1], misc_ss.at[6], misc_rs.at[6], sibling)
     serve(5, r3, -3)
     serve(6, l3, 3)
-    send_queries(3)
     arrived(gb, misc_rs.at[1])
     logits = jnp.concatenate([gb[...].astype(jnp.float32), jnp.zeros((32, TOKENS), jnp.float32)], axis=0)
     gate_of[...] = 1.0 / (1.0 + jnp.exp(-logits.T))
@@ -325,10 +324,13 @@
     arrived(qb.at[0], q_rs.at[0])
     early(0, 0)
     early(0, 1)
+    arrived(qb.at[1], q_rs.at[1])
+    early(1, 0)
     for i in range(CHUNKS):
         ring_arrived(4, i)
     serve(7, x4, 4)
-    for i in range(1, 4):
+    early(1, 1)
+    for i in range(2, 4):
         arrived(qb.at[i], q_rs.at[i])
         early(i, 0)
         early(i, 1)
@@ -351,6 +353,7 @@
     shard = pltpu.VMEM((16, SPAN, 2 * HEAD), bf16)
     anywhere = pl.BlockSpec(memory_space=pltpu.HBM)
     vmem = pl.BlockSpec(memory_space=pltpu.VMEM)
+    operands = queries[0], blocks, packed[0], fresh[0], gates[0].T, chosen[0]
     out = pl.pallas_call(
         kernel,
         out_shape=jax.ShapeDtypeStruct((TOKENS, WIDE), bf16),
@@ -385,9 +388,9 @@
             dma((4,)),
         ],
         compiler_params=pltpu.CompilerParams(
-            collective_id=1, has_side_effects=True, vmem_limit_bytes=56 * 2**20
+            collective_id=1, has_side_effects=True, vmem_limit_bytes=48 * 2**20
         ),
-    )(queries[0], blocks, packed[0], fresh[0], gates[0].T, chosen[0])
+    )(*(pltpu.with_memory_space_constraint(operand, pltpu.HBM) for operand in operands))
     return out[None]
 
 

time: 85.6 us -> 83.2 us (0.972)
  local copies, waits for them, and re-layouts: 2.29 us -> 0.97 us
  Pallas kernels: 82.2 us -> 81.2 us
    unnamed x1, local copies, waits for them, and re-layouts: 2.29 us -> 0.97 us
    pallas_call x1, Pallas kernels: 82.2 us -> 81.2 us  [per_device(): pl.pallas_call(kernel, out_shape=jax.ShapeDtypeStruct((TOKENS, WIDE), bf1...]
where the time goes in v4:
time: 83.2 us; the launch traced here: 82.2 us
  Pallas kernels  81.2 us (98%)
  local copies, waits for them, and re-layouts  0.97 us (1%)
    pallas_call x1, Pallas kernels, per_device(): pl.pallas_call(kernel, out_shape=jax.ShapeDtypeStruct((TOKENS, WIDE), bf1...  81.2 us

profile of v4, /device:TPU:32, one launch (start us, length us, event | category | flops | bytes accessed | tf_op | source)
XLA Modules:
  0.0 82.2 jit_solution(12036878304560445152)
XLA Ops:
  0.0 81.2 %shard_map.64 = bf16[128,4096]{1,0:T(8,128)(2,1)S(1)} custom-call(bf16[128,4096]{1,0:T(8,128)(2,1)} %bitcast.10, bf16[16,64,256]{2,1,0:T(8,128)(2,1)} %bitcast.11, bf16[2,16,256]{2,1,0:T(8,128)(2,1)} %bitcast.14, bf16[128,2,256]{2,1,0:T(2,128)(2,1)} %bitcast.12, bf16[96,128]{1,0:T(8,128)(2,1)} %bitcast.13, s32[2,2,16]{2,1,0:T(2,128)} %bitcast.15), custom_call_target="tpu_custom_call" | custom-call | tf_op jit(solution)/shard_map/pallas_call | solution.py:357
  81.2 1.0 %copy.8 = bf16[1,128,4096]{2,1,0:T(8,128)(2,1)} copy(bf16[1,128,4096]{2,1,0:T(8,128)(2,1)S(1)} %bitcast.9) | data formatting | bytes 2097152

commit v5 on v4

--- a/solution.py
+++ b/solution.py
@@ -124,7 +124,7 @@
         copy.start()
         pending.append(copy)
 
-    others = ((1, 0), (3, 0), (1, 1), (3, 1), (2, 0), (2, 1), (0, 1))
+    others = ((2, 0), (1, 0), (3, 0), (2, 1), (1, 1), (3, 1), (0, 1))
 
     def there(dx, dc):
         return lax.rem(x + dx + X, X) * C + lax.rem(c + dc, C)
@@ -188,7 +188,7 @@
     def early_unit(i, u):
         g = i // 2
         q = jnp.concatenate(
-            [qb[i, :, pl.ds(pl.multiple_of((2 * u + m) * HEAD, HEAD), HEAD)] for m in range(2)], axis=0
+            [qb[i, :, pl.ds((2 * u + m) * HEAD, HEAD)] for m in range(2)], axis=0
         )
         kv = pk[:, :, :, g].reshape(C * X * Z * 16, 2 * HEAD)
         scores = dot_nt(q, kv[:, :HEAD])
@@ -225,11 +225,8 @@
             )
 
     def early(i, half):
-        def body(u, carry):
-            early_unit(i, u)
-            return carry
-
-        lax.fori_loop(2 * half, 2 * half + 2, body, 0)
+        early_unit(i, 2 * half)
+        early_unit(i, 2 * half + 1)
 
     def late_unit(b, g, u):
         rows = slice(SPAN * b, SPAN * (b + 1))

time: 83.2 us -> 83.4 us (level)
  no operation moved by 1% of the time
where the time goes in v5:
time: 83.4 us; the launch traced here: 82.7 us
  Pallas kernels  81.7 us (98%)
  local copies, waits for them, and re-layouts  0.97 us (1%)
    pallas_call x1, Pallas kernels, per_device(): pl.pallas_call(kernel, out_shape=jax.ShapeDtypeStruct((TOKENS, WIDE), bf1...  81.7 us

profile of v5, /device:TPU:32, one launch (start us, length us, event | category | flops | bytes accessed | tf_op | source)
XLA Modules:
  0.0 82.7 jit_solution(9596619596238985790)
XLA Ops:
  0.0 81.7 %shard_map.64 = bf16[128,4096]{1,0:T(8,128)(2,1)S(1)} custom-call(bf16[128,4096]{1,0:T(8,128)(2,1)} %bitcast.10, bf16[16,64,256]{2,1,0:T(8,128)(2,1)} %bitcast.11, bf16[2,16,256]{2,1,0:T(8,128)(2,1)} %bitcast.14, bf16[128,2,256]{2,1,0:T(2,128)(2,1)} %bitcast.12, bf16[96,128]{1,0:T(8,128)(2,1)} %bitcast.13, s32[2,2,16]{2,1,0:T(2,128)} %bitcast.15), custom_call_target="tpu_custom_call" | custom-call | tf_op jit(solution)/shard_map/pallas_call | solution.py:354
  81.7 1.0 %copy.8 = bf16[1,128,4096]{2,1,0:T(8,128)(2,1)} copy(bf16[1,128,4096]{2,1,0:T(8,128)(2,1)S(1)} %bitcast.9) | data formatting | bytes 2097152
